TPU v7x, 32 devices: a whole 2x2x4 slice. The times are simulated.
32 devices in a mesh: groups: 2 (over y), node: 8 (over z, x), local: 2 (over core).
Axes of the slice: x: 2, y: 2, z: 4, core: 2. Of those that a mesh axis runs over, the one named last changes fastest.
Arguments:
- tokens: bfloat16 [2, 128, 7168], P(None, ('groups', 'node', 'local')), parts along dimension 1, may hold values from -6 to 6
- router: bfloat16 [7168, 16], replicated, may hold values from -0.25 to 0.25
- w_gate: bfloat16 [16, 7168, 2048], P('node', None, 'local'), may hold values from -0.0625 to 0.0625
- w_up: bfloat16 [16, 7168, 2048], P('node', None, 'local'), may hold values from -0.0625 to 0.0625
- w_down: bfloat16 [16, 2048, 7168], P('node', 'local'), may hold values from -0.25 to 0.25
- node_lists: int32 [2, 128, 4], P(None, ('groups', 'node', 'local')), parts along dimension 1, may hold values from 0 to 7, all different within a row; in each aligned block of 4 rows (0 to 3, 4 to 7, ..., all dimensions but the last counted through in order) at most 3 rows name the same one
Outputs:
- mixed: bfloat16 [2, 128, 7168], P(None, ('groups', 'node', 'local')), parts along dimension 1
There are 2 independent parts, one for each index of `groups`. A program takes and returns all parts, laid end to end along the dimension named above; an argument that names none is the same for every part. Nothing has to cross between parts.
Inputs may be any that keep to these rules, and one draw needn't show every extreme that they name: `node_lists`: each token names 4 distinct node groups. Among the 4 tokens of one device in one micro-batch no node group is named more than 3 times, and in some devices' tokens some group is named exactly 3 times.
All inputs are finite; a program needn't handle non-finite values.
Results may differ from a plain program's by a relative error of at most 0.009.
Values may be sent and summed in bfloat16 or wider, within the bound.
A program may use at most 192 MiB of HBM per device.

v0:
```python
import jax
import jax.numpy as jnp
from jax import lax
from jax.sharding import PartitionSpec as P

NODES_TOK = 4
SINK = 3


def expert_term(rows_in, gate_in, w_gate, w_up, w_down):
    pre_gate = jnp.einsum("rd,edh->erh", rows_in, w_gate, preferred_element_type=jnp.float32)
    pre_up = jnp.einsum("rd,edh->erh", rows_in, w_up, preferred_element_type=jnp.float32)
    weight_rows = jnp.transpose(gate_in).astype(jnp.float32)[:, :, None]
    hidden = (weight_rows * jax.nn.silu(pre_gate) * pre_up).astype(jnp.bfloat16)
    return jnp.einsum("erh,ehd->rd", hidden, w_down, preferred_element_type=jnp.float32)


def build_slots(chosen_int, capacity):
    before = jnp.cumsum(chosen_int, axis=1) - chosen_int
    slot_ids = jnp.arange(capacity, dtype=jnp.int32)
    marks = (before[..., None] == slot_ids).astype(jnp.int32) * chosen_int[..., None]
    return marks.astype(jnp.bfloat16)


def node_first(rows_in, gate_vals, slot_marks, w_gate, w_up, w_down):
    micro_count, tok_count, node_count, capacity = slot_marks.shape
    experts_here = w_gate.shape[0]
    gate_split = gate_vals.reshape(micro_count, tok_count, node_count, experts_here)
    send_rows = jnp.einsum(
        "btmc,btd->bmcd", slot_marks, rows_in, preferred_element_type=jnp.float32
    ).astype(jnp.bfloat16)
    send_gates = jnp.einsum(
        "btmc,btmi->bmci", slot_marks, gate_split, preferred_element_type=jnp.float32
    ).astype(jnp.bfloat16)
    recv_rows, recv_gates = (
        lax.all_to_all(send_rows, "node", split_axis=1, concat_axis=1, tiled=True),
        lax.all_to_all(send_gates, "node", split_axis=1, concat_axis=1, tiled=True),
    )
    flat_rows = micro_count * node_count * capacity
    all_rows, all_gates = (
        lax.all_gather(recv_rows.reshape(flat_rows, -1), "local", axis=0, tiled=True),
        lax.all_gather(recv_gates.reshape(flat_rows, experts_here), "local", axis=0, tiled=True),
    )
    summed = lax.psum_scatter(
        expert_term(all_rows, all_gates, w_gate, w_up, w_down).astype(jnp.bfloat16),
        "local",
        scatter_dimension=0,
        tiled=True,
    ).astype(jnp.float32)
    returned = lax.all_to_all(
        summed.reshape(micro_count, node_count, capacity, -1).astype(jnp.bfloat16),
        "node",
        split_axis=1,
        concat_axis=1,
        tiled=True,
    ).astype(jnp.float32)
    return jnp.einsum(
        "btmc,bmcd->btd", slot_marks.astype(jnp.float32), returned, precision=lax.Precision.HIGHEST
    )


def route_rows(rows_in, gate_vals, slot_marks, w_gate, w_up, w_down):
    result = node_first(rows_in, gate_vals, slot_marks, w_gate, w_up, w_down)
    return result


def local(tokens, router, w_gate, w_up, w_down, node_lists):
    micro_count, tok_count, model_width = tokens.shape
    node_count = lax.axis_size("node")
    expert_count = router.shape[1]
    capacity = min(tok_count, tok_count * NODES_TOK // node_count + max(1, tok_count // 4))
    logits = jnp.einsum("btd,de->bte", tokens, router, preferred_element_type=jnp.float32)
    scores = jax.nn.sigmoid(logits)
    for sweep in range(SINK):
        scores = scores / jnp.sum(scores, axis=2, keepdims=True)
        scores = scores / lax.psum(jnp.sum(scores, axis=1), ("node", "local"))[:, None, :]
    node_ids = jnp.arange(node_count, dtype=jnp.int32)
    chosen_int = jnp.sum((node_lists[..., None] == node_ids).astype(jnp.int32), axis=2)
    picked = jnp.repeat(chosen_int.astype(jnp.float32), expert_count // node_count, axis=2) * scores
    gate_vals = (picked / jnp.sum(picked, axis=2, keepdims=True)).astype(jnp.bfloat16)
    slot_marks = build_slots(chosen_int, capacity)
    outputs = []
    for micro in range(micro_count):
        outputs.append(
            route_rows(
                tokens[micro : micro + 1],
                gate_vals[micro : micro + 1],
                slot_marks[micro : micro + 1],
                w_gate,
                w_up,
                w_down,
            )
        )
    mixed = jnp.concatenate(outputs, axis=0)
    return mixed.astype(jnp.bfloat16)


def solution(mesh):
    return jax.shard_map(
        local,
        mesh=mesh,
        in_specs=(
            P(None, ("groups", "node", "local"), None),
            P(),
            P("node", None, "local"),
            P("node", None, "local"),
            P("node", "local", None),
            P(None, ("groups", "node", "local"), None),
        ),
        out_specs=P(None, ("groups", "node", "local"), None),
        check_vma=False,
    )
```

profile of v0, /device:TPU:0, one launch (start us, length us, event | category | flops | bytes accessed | tf_op | source)
XLA Modules:
  0.0 261.5 jit_solution(4423202399517368636)
XLA Ops:
  6.5 0.0 copy-start
  6.5 0.9 copy-done
  7.5 1.2 fusion.21
  8.7 0.1 divide_reduce_fusion.2
  8.8 34.9 %psum.21 = f32[2,16]{1,0:T(2,128)S(1)} all-reduce(f32[2,16]{1,0:T(2,128)S(1)} %get-tuple-element.13), channel_id=1, replica_groups=mesh['groups'=2,'node'=8,'local'=2] {'node','local'}, use_global_device_ids=true, to_apply=%region_4.0 | all-reduce | flops 32 | bytes 256 | tf_op jit(solution)/shard_map/psum | solution.py:76
  43.7 0.1 divide_reduce_fusion.1
  43.8 29.5 %psum.22 = f32[2,16]{1,0:T(2,128)S(1)} all-reduce(f32[2,16]{1,0:T(2,128)S(1)} %get-tuple-element.15), channel_id=1, replica_groups=mesh['groups'=2,'node'=8,'local'=2] {'node','local'}, use_global_device_ids=true, to_apply=%region_7.0 | all-reduce | flops 32 | bytes 256 | tf_op jit(solution)/shard_map/psum | solution.py:76
  73.3 0.1 divide_reduce_fusion
  73.4 29.5 %psum.23 = f32[2,16]{1,0:T(2,128)S(1)} all-reduce(f32[2,16]{1,0:T(2,128)S(1)} %get-tuple-element.17), channel_id=1, replica_groups=mesh['groups'=2,'node'=8,'local'=2] {'node','local'}, use_global_device_ids=true, to_apply=%region_10.0 | all-reduce | flops 32 | bytes 256 | tf_op jit(solution)/shard_map/psum | solution.py:76
  102.9 0.8 convert_reduce_fusion
  103.7 0.1 copy.77
  103.8 0.1 copy.78
  103.9 0.1 fusion.61
  104.0 0.1 divide_convert_fusion
  104.1 0.1 copy.79
  104.2 0.1 copy.80
  104.3 0.7 fusion.15
  105.0 3.3 %all-to-all-start = ((bf16[1,8,3,2]{2,3,0,1:T(2,128)(2,1)}), bf16[1,8,3,2]{2,3,0,1:T(2,128)(2,1)S(1)}, u32[]{:S(2)}, u32[]{:S(2)}) async-start(bf16[1,8,3,2]{2,3,0,1:T(2,128)(2,1)} %fusion.15), calls=%async_computation | async-start | bytes 8192 | tf_op jit(solution)/shard_map/all_to_all | solution.py:37
  108.4 0.1 copy.88
  108.5 0.1 copy.89
  108.6 0.7 fusion.16
  109.3 5.5 %all-to-all-done = bf16[1,8,3,2]{2,3,0,1:T(2,128)(2,1)S(1)} async-done(((bf16[1,8,3,2]{2,3,0,1:T(2,128)(2,1)}), bf16[1,8,3,2]{2,3,0,1:T(2,128)(2,1)S(1)}, u32[]{:S(2)}, u32[]{:S(2)}) %all-to-all-start) | async-done | bytes 128 | tf_op jit(solution)/shard_map/all_to_all | solution.py:37
  114.8 3.3 %all-to-all-start.3 = ((bf16[1,8,3,2]{2,3,0,1:T(2,128)(2,1)}), bf16[1,8,3,2]{2,3,0,1:T(2,128)(2,1)S(1)}, u32[]{:S(2)}, u32[]{:S(2)}) async-start(bf16[1,8,3,2]{2,3,0,1:T(2,128)(2,1)} %fusion.16), calls=%async_computation.4 | async-start | bytes 8192 | tf_op jit(solution)/shard_map/all_to_all | solution.py:37
  118.1 1.1 fusion.5
  119.2 1.1 copy.85
  120.3 4.1 %all-to-all-done.3 = bf16[1,8,3,2]{2,3,0,1:T(2,128)(2,1)S(1)} async-done(((bf16[1,8,3,2]{2,3,0,1:T(2,128)(2,1)}), bf16[1,8,3,2]{2,3,0,1:T(2,128)(2,1)S(1)}, u32[]{:S(2)}, u32[]{:S(2)}) %all-to-all-start.3) | async-done | bytes 128 | tf_op jit(solution)/shard_map/all_to_all | solution.py:37
  124.4 3.5 %all-to-all-start.1 = ((bf16[1,8,3,7168]{3,2,0,1:T(4,128)(2,1)}), bf16[1,8,3,7168]{3,2,0,1:T(4,128)(2,1)S(1)}, u32[]{:S(2)}, u32[]{:S(2)}) async-start(bf16[1,8,3,7168]{3,2,0,1:T(4,128)(2,1)} %copy.85), calls=%async_computation.1 | async-start | bytes 917504 | tf_op jit(solution)/shard_map/all_to_all | solution.py:36
  127.9 1.1 fusion.6
  129.0 1.1 copy.94
  130.1 0.1 reshape.120
  130.2 0.1 reshape.122
  130.3 1.8 all-gather
  132.1 1.8 all-gather.1
  133.8 0.1 reshape.124
  133.9 0.1 reshape.125
  134.0 4.9 %all-to-all-done.1 = bf16[1,8,3,7168]{3,2,0,1:T(4,128)(2,1)S(1)} async-done(((bf16[1,8,3,7168]{3,2,0,1:T(4,128)(2,1)}), bf16[1,8,3,7168]{3,2,0,1:T(4,128)(2,1)S(1)}, u32[]{:S(2)}, u32[]{:S(2)}) %all-to-all-start.1) | async-done | bytes 344096 | tf_op jit(solution)/shard_map/all_to_all | solution.py:36
  138.9 3.7 %all-to-all-start.4 = ((bf16[1,8,3,7168]{3,2,0,1:T(4,128)(2,1)}), bf16[1,8,3,7168]{3,2,0,1:T(4,128)(2,1)S(1)}, u32[]{:S(2)}, u32[]{:S(2)}) async-start(bf16[1,8,3,7168]{3,2,0,1:T(4,128)(2,1)} %copy.94), calls=%async_computation.5 | async-start | bytes 917504 | tf_op jit(solution)/shard_map/all_to_all | solution.py:36
  142.6 0.0 reduce-scatter.3.cloned.1.call-start
  142.6 0.3 reshape.112
  142.9 2.3 all_gather.13
  145.2 11.9 %convolution_bitcast_fusion.7 = f32[2,48,1024]{2,1,0:T(8,128)S(1)} fusion(bf16[2,7168,1024]{2,1,0:T(8,128)(2,1)} %param.8, bf16[48,7168]{1,0:T(8,128)(2,1)S(1)} %all_gather.13), kind=kOutput, calls=%fused_computation.20 | convolution fusion | flops 1409286144 | bytes 30441472 | tf_op jit(solution)/shard_map/rd,edh->erh/dot_general | solution.py:11
  157.1 21.7 %fusion.3 = bf16[48,7168]{1,0:T(8,128)(2,1)} fusion(bf16[2,1024,7168]{2,1,0:T(8,128)(2,1)} %param.10, bf16[2,7168,1024]{2,1,0:T(8,128)(2,1)} %param.9, bf16[48,7168]{1,0:T(8,128)(2,1)S(1)} %all_gather.13, f32[2,48,1024]{2,1,0:T(8,128)S(1)} %convolution_bitcast_fusion.7, f32[2,48]{1,0:T(2,128)S(1)} %bitcast.129), kind=kOutput, calls=%fused_computation.5 | convolution fusion | flops 2819604480 | bytes 60490112 | tf_op jit(solution)/shard_map/erh,ehd->rd/dot_general | solution.py:15
  178.8 0.0 reduce-scatter.3.cloned.1.call-update
  178.8 0.0 reduce-scatter.5.cloned.1.call-start
  178.8 0.0 all-to-all-done.4
  178.9 0.3 reshape.118
  179.2 2.3 all_gather.15
  181.5 12.2 %convolution_bitcast_fusion.5 = f32[2,48,1024]{2,1,0:T(8,128)S(1)} fusion(bf16[2,7168,1024]{2,1,0:T(8,128)(2,1)} %param.8, bf16[48,7168]{1,0:T(8,128)(2,1)S(1)} %all_gather.15), kind=kOutput, calls=%fused_computation.18 | convolution fusion | flops 1409286144 | bytes 30441472 | tf_op jit(solution)/shard_map/rd,edh->erh/dot_general | solution.py:11
  193.7 0.0 copy-start.1
  193.7 21.7 %fusion.4 = bf16[48,7168]{1,0:T(8,128)(2,1)} fusion(bf16[2,1024,7168]{2,1,0:T(8,128)(2,1)} %param.10, bf16[2,7168,1024]{2,1,0:T(8,128)(2,1)} %param.9, bf16[48,7168]{1,0:T(8,128)(2,1)S(1)} %all_gather.15, f32[2,48,1024]{2,1,0:T(8,128)S(1)} %convolution_bitcast_fusion.5, f32[2,48]{1,0:T(2,128)S(1)} %bitcast.128), kind=kOutput, calls=%fused_computation.6 | convolution fusion | flops 2819604480 | bytes 60490112 | tf_op jit(solution)/shard_map/erh,ehd->rd/dot_general | solution.py:15
  215.4 0.0 reduce-scatter.5.cloned.1.call-update
  215.4 0.0 reduce-scatter.3.cloned.1.call-done
  215.5 1.9 convert_element_type.104
  217.4 6.0 %all-to-all-start.2 = ((bf16[1,8,3,7168]{3,2,0,1:T(4,128)(2,1)}), bf16[1,8,3,7168]{3,2,0,1:T(4,128)(2,1)S(1)}, u32[]{:S(2)}, u32[]{:S(2)}) async-start(bf16[1,8,3,7168]{3,2,0,1:T(4,128)(2,1)} %bitcast.13), calls=%async_computation.3 | async-start | bytes 917504 | tf_op jit(solution)/shard_map/all_to_all | solution.py:50
  223.4 1.8 reduce-scatter.5.cloned.1.call-done
  225.1 2.0 convert_element_type.113
  227.1 9.7 %all-to-all-done.2 = bf16[1,8,3,7168]{3,2,0,1:T(4,128)(2,1)S(1)} async-done(((bf16[1,8,3,7168]{3,2,0,1:T(4,128)(2,1)}), bf16[1,8,3,7168]{3,2,0,1:T(4,128)(2,1)S(1)}, u32[]{:S(2)}, u32[]{:S(2)}) %all-to-all-start.2) | async-done | bytes 344096 | tf_op jit(solution)/shard_map/all_to_all | solution.py:50
  236.8 3.6 %all-to-all-start.5 = ((bf16[1,8,3,7168]{3,2,0,1:T(4,128)(2,1)}), bf16[1,8,3,7168]{3,2,0,1:T(4,128)(2,1)S(1)}, u32[]{:S(2)}, u32[]{:S(2)}) async-start(bf16[1,8,3,7168]{3,2,0,1:T(4,128)(2,1)} %bitcast.28), calls=%async_computation.7 | async-start | bytes 917504 | tf_op jit(solution)/shard_map/all_to_all | solution.py:50
  240.4 0.3 fusion.10
  240.6 13.0 %all-to-all-done.5 = bf16[1,8,3,7168]{3,2,0,1:T(4,128)(2,1)S(1)} async-done(((bf16[1,8,3,7168]{3,2,0,1:T(4,128)(2,1)}), bf16[1,8,3,7168]{3,2,0,1:T(4,128)(2,1)S(1)}, u32[]{:S(2)}, u32[]{:S(2)}) %all-to-all-start.5) | async-done | bytes 344096 | tf_op jit(solution)/shard_map/all_to_all | solution.py:50
  253.7 0.3 fusion.9
  253.9 0.7 pad_maximum_fusion
  254.6 0.0 copy-done.1
  (10 shorter events, 0.1 us)
Async XLA Ops:
  6.5 0.9 copy-start
  105.0 9.7 %all-to-all-start = ((bf16[1,8,3,2]{2,3,0,1:T(2,128)(2,1)}), bf16[1,8,3,2]{2,3,0,1:T(2,128)(2,1)S(1)}, u32[]{:S(2)}, u32[]{:S(2)}) async-start(bf16[1,8,3,2]{2,3,0,1:T(2,128)(2,1)} %fusion.15), calls=%async_computation | async-start | bytes 8192 | tf_op jit(solution)/shard_map/all_to_all | solution.py:37
  114.8 9.6 %all-to-all-start.3 = ((bf16[1,8,3,2]{2,3,0,1:T(2,128)(2,1)}), bf16[1,8,3,2]{2,3,0,1:T(2,128)(2,1)S(1)}, u32[]{:S(2)}, u32[]{:S(2)}) async-start(bf16[1,8,3,2]{2,3,0,1:T(2,128)(2,1)} %fusion.16), calls=%async_computation.4 | async-start | bytes 8192 | tf_op jit(solution)/shard_map/all_to_all | solution.py:37
  124.4 14.5 %all-to-all-start.1 = ((bf16[1,8,3,7168]{3,2,0,1:T(4,128)(2,1)}), bf16[1,8,3,7168]{3,2,0,1:T(4,128)(2,1)S(1)}, u32[]{:S(2)}, u32[]{:S(2)}) async-start(bf16[1,8,3,7168]{3,2,0,1:T(4,128)(2,1)} %copy.85), calls=%async_computation.1 | async-start | bytes 917504 | tf_op jit(solution)/shard_map/all_to_all | solution.py:36
  138.9 39.9 %all-to-all-start.4 = ((bf16[1,8,3,7168]{3,2,0,1:T(4,128)(2,1)}), bf16[1,8,3,7168]{3,2,0,1:T(4,128)(2,1)S(1)}, u32[]{:S(2)}, u32[]{:S(2)}) async-start(bf16[1,8,3,7168]{3,2,0,1:T(4,128)(2,1)} %copy.94), calls=%async_computation.5 | async-start | bytes 917504 | tf_op jit(solution)/shard_map/all_to_all | solution.py:36
  142.6 72.9 %reduce-scatter.3.cloned.1.call-start = ((), (), s32[]{:S(2)}) async-start(), calls=%async_computation.8 | async-start | bytes 1032192 | tf_op jit(solution)/shard_map/reduce_scatter | solution.py:44
  178.8 46.3 %reduce-scatter.5.cloned.1.call-start = ((), (), s32[]{:S(2)}) async-start(), calls=%async_computation.9 | async-start | bytes 1032192 | tf_op jit(solution)/shard_map/reduce_scatter | solution.py:44
  193.7 61.0 %copy-start.1 = (bf16[7168,16]{0,1:T(8,128)(2,1)S(1)}, bf16[7168,16]{0,1:T(8,128)(2,1)}, u32[]{:S(2)}) copy-start(bf16[7168,16]{0,1:T(8,128)(2,1)} %param.7) | copy-start | bytes 688132
  217.4 19.3 %all-to-all-start.2 = ((bf16[1,8,3,7168]{3,2,0,1:T(4,128)(2,1)}), bf16[1,8,3,7168]{3,2,0,1:T(4,128)(2,1)S(1)}, u32[]{:S(2)}, u32[]{:S(2)}) async-start(bf16[1,8,3,7168]{3,2,0,1:T(4,128)(2,1)} %bitcast.13), calls=%async_computation.3 | async-start | bytes 917504 | tf_op jit(solution)/shard_map/all_to_all | solution.py:50
  236.8 16.9 %all-to-all-start.5 = ((bf16[1,8,3,7168]{3,2,0,1:T(4,128)(2,1)}), bf16[1,8,3,7168]{3,2,0,1:T(4,128)(2,1)S(1)}, u32[]{:S(2)}, u32[]{:S(2)}) async-start(bf16[1,8,3,7168]{3,2,0,1:T(4,128)(2,1)} %bitcast.28), calls=%async_computation.7 | async-start | bytes 917504 | tf_op jit(solution)/shard_map/all_to_all | solution.py:50
Sparse Core Ops, SparseCore 0:
  178.9 9.5 reduce-scatter.2
  215.6 9.5 reduce-scatter.4
where the time goes:
time: 262 us; the launch traced here: 261 us
  blocking collectives  102 us (39%)
  matrix products  72.9 us (28%)
  waiting for transfers between devices  39 us (15%)
  starting transfers between devices  23.5 us (9%)
  between operations  13.5 us (5%)
  local copies, waits for them, and re-layouts  8.58 us (3%)
    psum x3, blocking collectives, local(): lax.psum(jnp.sum(scores, axis=1), ('node', 'local'))[:, None, :]  93.9 us
    dot_general x2, matrix products, expert_term(): jnp.einsum('erh,ehd->rd', hidden, w_down, preferred_element_type=jnp.floa...  43.4 us
    dot_general x2, matrix products, expert_term(): jnp.einsum('rd,edh->erh', rows_in, w_gate, preferred_element_type=jnp.flo...  24.1 us
    all_to_all x2, waiting for transfers between devices, node_first(): lax.all_to_all(summed.reshape(micro_count, node_count, capacity, -1).asty...  22.7 us
    all_to_all x2, starting transfers between devices, node_first(): lax.all_to_all(summed.reshape(micro_count, node_count, capacity, -1).asty...  9.59 us
    all_to_all x2, waiting for transfers between devices, node_first(): lax.all_to_all(send_gates, 'node', split_axis=1, concat_axis=1, tiled=True)  9.59 us
    all_to_all x2, starting transfers between devices, node_first(): lax.all_to_all(send_rows, 'node', split_axis=1, concat_axis=1, tiled=True)  7.13 us
    all_to_all x2, starting transfers between devices, node_first(): lax.all_to_all(send_gates, 'node', split_axis=1, concat_axis=1, tiled=True)  6.64 us
  transfers between devices with their start and end apart: 8, of which 6 were waited for; matrix products, arithmetic and copies ran while one was open for 30% of the time, Pallas kernels for 0%

commit v1 on v0

--- a/solution.py
+++ b/solution.py
@@ -1,6 +1,8 @@
 import jax
 import jax.numpy as jnp
 from jax import lax
+from jax.experimental import pallas as pl
+from jax.experimental.pallas import tpu as pltpu
 from jax.sharding import PartitionSpec as P
 
 NODES_TOK = 4
@@ -95,9 +97,338 @@
     return mixed.astype(jnp.bfloat16)
 
 
+MESH = pl.DeviceIdType.MESH
+BLK = 1024
+PAIRS = 12
+
+
+def fused_kernel(
+    tok_ref, list_ref, router_hbm, gate_hbm, up_hbm, down_hbm, out_ref,
+    wbuf, router_buf, xg, mg, xs, acc, hid, part, sib_in, mid, x_in, fin, z_in,
+    w_sem, router_sem, gz_send, gz_recv, gx_send, gx_recv, gs_send, gs_recv,
+    rs_send, rs_recv, rx_send, rx_recv, rz_send, rz_recv,
+):
+    width = tok_ref.shape[2]
+    chunks = width // BLK
+    experts_here = gate_hbm.shape[0]
+    zs = xg.shape[3]
+    half = BLK // 2
+    grp, node, core = lax.axis_index("groups"), lax.axis_index("node"), lax.axis_index("local")
+    zi, xi = node // 2, node % 2
+    sib = (grp, node, 1 - core)
+    xnb = (grp, zi * 2 + (1 - xi), core)
+
+    def z_at(step):
+        return (zi + step) % zs
+
+    def znb(step):
+        return (grp, z_at(step) * 2 + xi, core)
+
+    def first_copy(pair, slot, kind):
+        k, e = pair // 2, pair % 2
+        rows = pl.ds(pl.multiple_of(k * BLK, BLK), BLK)
+        source = (gate_hbm, up_hbm)[kind].at[e, rows, :]
+        return pltpu.make_async_copy(source, wbuf.at[slot, kind], w_sem.at[slot, kind])
+
+    def down_copies(q, slot):
+        cols = pl.ds(pl.multiple_of(q * BLK, BLK), BLK)
+        return (
+            pltpu.make_async_copy(down_hbm.at[0, :, cols], wbuf.at[slot, 0], w_sem.at[slot, 0]),
+            pltpu.make_async_copy(down_hbm.at[1, :, cols], wbuf.at[slot, 1], w_sem.at[slot, 1]),
+        )
+
+    router_copy = pltpu.make_async_copy(router_hbm, router_buf, router_sem)
+    router_copy.start()
+
+    @pl.loop(0, PAIRS)
+    def _(pair):
+        for kind in range(2):
+            first_copy(pair, pair, kind).start()
+
+    rows_own = jnp.concatenate(
+        [tok_ref[0].astype(jnp.float32), tok_ref[1].astype(jnp.float32)], axis=0
+    )
+    for k in range(chunks):
+        left = rows_own[:, k * BLK : k * BLK + half]
+        right = rows_own[:, k * BLK + half : (k + 1) * BLK]
+        xg[k, core, xi, zi] = jnp.concatenate([left, right], axis=0).astype(jnp.bfloat16)
+
+    barrier = pltpu.get_barrier_semaphore()
+    peers = [sib, xnb] + [znb(step) for step in range(1, zs)]
+    for peer in peers:
+        pl.semaphore_signal(barrier, inc=1, device_id=peer, device_id_type=MESH)
+    pl.semaphore_wait(barrier, len(peers))
+
+    def remote(src, dst, send, recv, peer):
+        return pltpu.make_async_remote_copy(
+            src_ref=src, dst_ref=dst, send_sem=send, recv_sem=recv, device_id=peer, device_id_type=MESH
+        )
+
+    def slot_of(k):
+        return mg if k is None else xg.at[k]
+
+    def sem_of(k):
+        return chunks if k is None else k
+
+    def gather_z(k, step):
+        place = slot_of(k).at[core, xi, zi]
+        return remote(place, place, gz_send.at[sem_of(k), step - 1], gz_recv.at[sem_of(k), step - 1], znb(step))
+
+    def gather_x(k):
+        place = slot_of(k).at[core, xi]
+        return remote(place, place, gx_send.at[sem_of(k)], gx_recv.at[sem_of(k)], xnb)
+
+    def gather_s(k):
+        place = slot_of(k).at[core]
+        return remote(place, place, gs_send.at[sem_of(k)], gs_recv.at[sem_of(k)], sib)
+
+    def start_z(k):
+        for step in range(1, zs):
+            gather_z(k, step).start()
+
+    def relay_x(k):
+        for step in range(1, zs):
+            gather_z(k, step).wait_recv()
+        gather_x(k).start()
+
+    def relay_s(k):
+        gather_x(k).wait_recv()
+        gather_s(k).start()
+
+    @pl.loop(0, chunks)
+    def _(k):
+        start_z(k)
+
+    router_copy.wait()
+    logits = jnp.dot(rows_own.astype(jnp.bfloat16), router_buf[...], preferred_element_type=jnp.float32)
+    experts = logits.shape[1]
+    logits = jnp.concatenate([logits, jnp.zeros((logits.shape[0], 128 - experts), jnp.float32)], axis=1)
+    marks = []
+    group_of = lax.broadcasted_iota(jnp.int32, (tok_ref.shape[1], 128), 1) // experts_here
+    for b in range(2):
+        names = list_ref[b]
+        total = jnp.zeros(group_of.shape, jnp.float32)
+        for j in range(names.shape[1]):
+            total = total + (names[:, j : j + 1] == group_of).astype(jnp.float32)
+        marks.append(total)
+    mg[core, xi, zi] = jnp.concatenate([logits] + marks, axis=0)
+    start_z(None)
+
+    relay_x(0)
+
+    @pl.loop(1, chunks)
+    def _(k):
+        relay_x(k)
+        relay_s(k - 1)
+
+    relay_x(None)
+    relay_s(chunks - 1)
+    relay_s(None)
+
+    rows = 2 * 2 * zs * 8
+    acc[...] = jnp.zeros_like(acc)
+
+    @pl.loop(0, chunks * 2)
+    def _(pair):
+        k, e = pair // 2, pair % 2
+        slot = pair % PAIRS
+
+        @pl.when(e == 0)
+        def _():
+            gather_s(k).wait_recv()
+            wide = xg[k].astype(jnp.float32).reshape(2 * 2 * zs, 16, half)
+            xs[:, :half] = wide[:, :8].reshape(rows, half).astype(jnp.bfloat16)
+            xs[:, half:] = wide[:, 8:].reshape(rows, half).astype(jnp.bfloat16)
+
+        for kind in range(2):
+            first_copy(pair, slot, kind).wait()
+
+            @pl.loop(0, BLK // 256)
+            def _(n):
+                cols = pl.ds(pl.multiple_of(n * 256, 256), 256)
+                acc[e, kind, :, cols] += jnp.dot(
+                    xs[...], wbuf[slot, kind, :, cols], preferred_element_type=jnp.float32
+                )
+
+        later = pair + PAIRS
+
+        @pl.when(later < chunks * 2)
+        def _():
+            for kind in range(2):
+                first_copy(later, slot, kind).start()
+
+        @pl.when((later >= chunks * 2) & (later < chunks * 3))
+        def _():
+            for copy in down_copies(later - chunks * 2, slot):
+                copy.start()
+
+    gather_s(None).wait_recv()
+    meta = mg[...].reshape(2 * 2 * zs, 16, 128)
+    lane = lax.broadcasted_iota(jnp.int32, (rows, 128), 1)
+    real = lane < experts
+    first = (lax.broadcasted_iota(jnp.int32, (rows, 128), 0) // 4) % 2 == 0
+    scores = 1.0 / (1.0 + jnp.exp(-meta[:, :8].reshape(rows, 128)))
+    scores = jnp.where(real, scores, 0.0)
+    for sweep in range(SINK):
+        scores = scores / jnp.sum(scores, axis=1, keepdims=True)
+        sum_a = jnp.sum(jnp.where(first, scores, 0.0), axis=0, keepdims=True)
+        sum_b = jnp.sum(jnp.where(first, 0.0, scores), axis=0, keepdims=True)
+        scores = scores / jnp.where(real, jnp.where(first, sum_a, sum_b), 1.0)
+    picked = meta[:, 8:].reshape(rows, 128) * scores
+    gates = (picked / jnp.sum(picked, axis=1, keepdims=True)).astype(jnp.bfloat16).astype(jnp.float32)
+    for e in range(experts_here):
+        weight = jnp.sum(jnp.where(lane == node * experts_here + e, gates, 0.0), axis=1, keepdims=True)
+
+        @pl.loop(0, BLK // 256)
+        def _(n):
+            cols = pl.ds(pl.multiple_of(n * 256, 256), 256)
+            pre = acc[e, 0, :, cols]
+            hid[e, :, cols] = (weight * (pre / (1.0 + jnp.exp(-pre))) * acc[e, 1, :, cols]).astype(jnp.bfloat16)
+
+    def reduce_s(q):
+        return remote(part.at[q, 1 - core], sib_in.at[q], rs_send.at[q], rs_recv.at[q], sib)
+
+    def reduce_x(q):
+        return remote(mid.at[q, 1 - xi], x_in.at[q], rx_send.at[q], rx_recv.at[q], xnb)
+
+    def reduce_z(q, step):
+        return remote(
+            fin.at[q, z_at(step)], z_in.at[q, step - 1], rz_send.at[q, step - 1], rz_recv.at[q, step - 1], znb(step)
+        )
+
+    def multiply(q):
+        slot = (chunks * 2 + q) % PAIRS
+        for copy in down_copies(q, slot):
+            copy.wait()
+        for side in range(2):
+            for n in range(half // 256):
+                cols = slice(side * half + n * 256, side * half + (n + 1) * 256)
+                value = jnp.dot(hid[0], wbuf[slot, 0, :, cols], preferred_element_type=jnp.float32)
+                value = value + jnp.dot(hid[1], wbuf[slot, 1, :, cols], preferred_element_type=jnp.float32)
+                acc[0, side, :, n * 256 : (n + 1) * 256] = value
+        low = acc[0, 0, :, :half].reshape(2 * 2 * zs, 8, half)
+        high = acc[0, 1, :, :half].reshape(2 * 2 * zs, 8, half)
+        part[q] = jnp.concatenate([low, high], axis=1).reshape(2, 2, zs, 16, half).astype(jnp.bfloat16)
+        reduce_s(q).start()
+
+    def add_pair(q):
+        reduce_s(q).wait_recv()
+        mid[q] = (part[q, core].astype(jnp.float32) + sib_in[q].astype(jnp.float32)).astype(jnp.bfloat16)
+        reduce_x(q).start()
+
+    def add_x(q):
+        reduce_x(q).wait_recv()
+        fin[q] = (mid[q, xi].astype(jnp.float32) + x_in[q].astype(jnp.float32)).astype(jnp.bfloat16)
+        for step in range(1, zs):
+            reduce_z(q, step).start()
+
+    def add_z(q):
+        total = fin[q, zi].astype(jnp.float32)
+        for step in range(1, zs):
+            reduce_z(q, step).wait_recv()
+            total = total + z_in[q, step - 1].astype(jnp.float32)
+        for side in range(2):
+            cols = pl.ds(pl.multiple_of(q * BLK + side * half, half), half)
+            for b in range(2):
+                row = side * 8 + b * 4
+                out_ref[b, :, cols] = total[row : row + 4].astype(jnp.bfloat16)
+
+    @pl.loop(0, chunks + 3)
+    def _(q):
+        @pl.when(q < chunks)
+        def _():
+            multiply(q)
+
+        @pl.when((q >= 1) & (q < chunks + 1))
+        def _():
+            add_pair(q - 1)
+
+        @pl.when((q >= 2) & (q < chunks + 2))
+        def _():
+            add_x(q - 2)
+
+        @pl.when(q >= 3)
+        def _():
+            add_z(q - 3)
+
+    @pl.loop(0, chunks)
+    def _(k):
+        for step in range(1, zs):
+            gather_z(k, step).wait_send()
+            reduce_z(k, step).wait_send()
+        gather_x(k).wait_send()
+        gather_s(k).wait_send()
+        reduce_s(k).wait_send()
+        reduce_x(k).wait_send()
+
+    for step in range(1, zs):
+        gather_z(None, step).wait_send()
+    gather_x(None).wait_send()
+    gather_s(None).wait_send()
+
+
+def fused(tokens, router, w_gate, w_up, w_down, node_lists):
+    width = tokens.shape[2]
+    chunks = width // BLK
+    zs = lax.axis_size("node") // 2
+    half = BLK // 2
+    rows = 2 * 2 * zs * 8
+    bf16, f32 = jnp.bfloat16, jnp.float32
+    dma = pltpu.SemaphoreType.DMA
+    any_spec = pl.BlockSpec(memory_space=pl.ANY)
+    vmem_spec = pl.BlockSpec(memory_space=pltpu.VMEM)
+    return pl.pallas_call(
+        fused_kernel,
+        out_shape=jax.ShapeDtypeStruct(tokens.shape, tokens.dtype),
+        in_specs=[vmem_spec, vmem_spec, any_spec, any_spec, any_spec, any_spec],
+        out_specs=vmem_spec,
+        scratch_shapes=[
+            pltpu.VMEM((PAIRS, 2, BLK, BLK), bf16),
+            pltpu.VMEM(router.shape, bf16),
+            pltpu.VMEM((chunks, 2, 2, zs, 16, half), bf16),
+            pltpu.VMEM((2, 2, zs, 16, 128), f32),
+            pltpu.VMEM((rows, BLK), bf16),
+            pltpu.VMEM((2, 2, rows, BLK), f32),
+            pltpu.VMEM((2, rows, BLK), bf16),
+            pltpu.VMEM((chunks, 2, 2, zs, 16, half), bf16),
+            pltpu.VMEM((chunks, 2, zs, 16, half), bf16),
+            pltpu.VMEM((chunks, 2, zs, 16, half), bf16),
+            pltpu.VMEM((chunks, zs, 16, half), bf16),
+            pltpu.VMEM((chunks, zs, 16, half), bf16),
+            pltpu.VMEM((chunks, zs - 1, 16, half), bf16),
+            dma((PAIRS, 2)),
+            dma,
+            dma((chunks + 1, zs - 1)), dma((chunks + 1, zs - 1)),
+            dma((chunks + 1,)), dma((chunks + 1,)),
+            dma((chunks + 1,)), dma((chunks + 1,)),
+            dma((chunks,)), dma((chunks,)),
+            dma((chunks,)), dma((chunks,)),
+            dma((chunks, zs - 1)), dma((chunks, zs - 1)),
+        ],
+        compiler_params=pltpu.CompilerParams(
+            collective_id=0, has_side_effects=True, vmem_limit_bytes=63 * 1024 * 1024
+        ),
+        cost_estimate=pl.CostEstimate(
+            flops=12 * rows * width * BLK, bytes_accessed=12 * width * BLK, transcendentals=2 * rows * BLK
+        ),
+    )(tokens, node_lists, router, w_gate, w_up, w_down)
+
+
 def solution(mesh):
+    def body(tokens, router, w_gate, w_up, w_down, node_lists):
+        fits = (
+            mesh.shape["local"] == 2
+            and mesh.shape["node"] % 2 == 0
+            and tokens.shape[:2] == (2, 4)
+            and w_gate.shape[0] == 2
+            and w_gate.shape[2] == BLK
+            and tokens.shape[2] % BLK == 0
+        )
+        plan = fused if fits else local
+        return plan(tokens, router, w_gate, w_up, w_down, node_lists)
+
     return jax.shard_map(
-        local,
+        body,
         mesh=mesh,
         in_specs=(
             P(None, ("groups", "node", "local"), None),

time: 262 us -> 88.2 us (0.34)
  blocking collectives: 102 us -> 0 us
  Pallas kernels: 0 us -> 83.9 us
  matrix products: 72.9 us -> 0 us
  waiting for transfers between devices: 39 us -> 0 us
  starting transfers between devices: 23.5 us -> 0 us
  between operations: 13.5 us -> 0.01 us
  local copies, waits for them, and re-layouts: 8.58 us -> 4.09 us
    psum x3 -> x0, blocking collectives: 93.9 us -> none  [local(): lax.psum(jnp.sum(scores, axis=1), ('node', 'local'))[:, None, :]]
    pallas_call x0 -> x1, Pallas kernels: none -> 83.9 us  [fused(): pl.pallas_call(fused_kernel, out_shape=jax.ShapeDtypeStruct(tokens.shape,...]
    dot_general x11 -> x0, matrix products: 72.9 us -> none  [the longest x2 43.4 us: expert_term(): jnp.einsum('erh,ehd->rd', hidden, w_down, preferred_element_type=jnp.floa...]
    all_to_all x6 -> x0, waiting for transfers between devices: 37.2 us -> none  [the longest x2 22.7 us: node_first(): lax.all_to_all(summed.reshape(micro_count, node_count, capacity, -1).asty...]
    all_to_all x6 -> x0, starting transfers between devices: 23.4 us -> none  [the longest x2 9.59 us: node_first(): lax.all_to_all(summed.reshape(micro_count, node_count, capacity, -1).asty...]
    all_gather x4 -> x0, blocking collectives: 8.11 us -> none  [the longest x2 4.6 us: node_first(): lax.all_gather(recv_rows.reshape(flat_rows, -1), 'local', axis=0, tiled=T...]
    convert_element_type x9 -> x0, local copies, waits for them, and re-layouts: 6.31 us -> none  [the longest x2 3.89 us: node_first(): summed.reshape(micro_count, node_count, capacity, -1).astype(jnp.bfloat16)]
    unnamed x6 -> x2, local copies, waits for them, and re-layouts: 1.13 us -> 4.09 us
  transfers between devices with their start and end apart: 8 -> 0, of which waited for: 6 -> 0; matrix products, arithmetic and copies ran while one was open for 30% -> 0% of each run, Pallas kernels for 0% -> 0%
where the time goes in v1:
time: 88.2 us; the launch traced here: 88 us
  Pallas kernels  83.9 us (95%)
  local copies, waits for them, and re-layouts  4.09 us (5%)
    pallas_call x1, Pallas kernels, fused(): pl.pallas_call(fused_kernel, out_shape=jax.ShapeDtypeStruct(tokens.shape,...  83.9 us
    unnamed x2, local copies, waits for them, and re-layouts  4.09 us

profile of v1, /device:TPU:0, one launch (start us, length us, event | category | flops | bytes accessed | tf_op | source)
XLA Modules:
  0.0 88.0 jit_solution(720650779669775863)
XLA Ops:
  0.0 2.5 %copy.7.router_hbm = bf16[7168,16]{1,0:T(8,128)(2,1)} copy(bf16[7168,16]{0,1:T(8,128)(2,1)} %param.7) | data formatting | bytes 458752 | tf_op args[1]
  2.5 83.9 %shard_map.64 = bf16[2,4,7168]{2,1,0:T(4,128)(2,1)} custom-call(bf16[2,4,7168]{2,1,0:T(4,128)(2,1)} %tok_ref.1, s32[2,4,4]{2,1,0:T(4,128)} %list_ref.1, bf16[7168,16]{1,0:T(8,128)(2,1)} %copy.7.router_hbm, bf16[2,7168,1024]{2,1,0:T(8,128)(2,1)} %gate_hbm.1, bf16[2,7168,1024]{2,1,0:T(8,128)(2,1)} %up_hbm.1, bf16[2,1024,7168]{2,1,0:T(8,128)(2,1)} %down_hbm.1), custom_call_target="tpu_custom_call" | custom-call | flops 11274289152 | bytes 88080384 | tf_op jit(solution)/shard_map/pallas_call | solution.py:380
  86.4 1.6 %copy.9 = bf16[2,4,7168]{2,1,0:T(4,128)(2,1)} copy(bf16[2,4,7168]{2,1,0:T(4,128)(2,1)} %shard_map.64) | data formatting | bytes 229376

commit v2 on v1

--- a/solution.py
+++ b/solution.py
@@ -195,12 +195,13 @@
         gather_x(k).wait_recv()
         gather_s(k).start()
 
-    @pl.loop(0, chunks)
-    def _(k):
-        start_z(k)
+    start_z(0)
+    start_z(1)
 
     router_copy.wait()
-    logits = jnp.dot(rows_own.astype(jnp.bfloat16), router_buf[...], preferred_element_type=jnp.float32)
+    logits = lax.dot_general(
+        rows_own.astype(jnp.bfloat16), router_buf[...], (((1,), (1,)), ((), ())), preferred_element_type=jnp.float32
+    )
     experts = logits.shape[1]
     logits = jnp.concatenate([logits, jnp.zeros((logits.shape[0], 128 - experts), jnp.float32)], axis=1)
     marks = []
@@ -215,15 +216,11 @@
     start_z(None)
 
     relay_x(0)
-
-    @pl.loop(1, chunks)
-    def _(k):
-        relay_x(k)
-        relay_s(k - 1)
-
+    start_z(2)
+    relay_x(1)
+    start_z(3)
+    relay_s(0)
     relay_x(None)
-    relay_s(chunks - 1)
-    relay_s(None)
 
     rows = 2 * 2 * zs * 8
     acc[...] = jnp.zeros_like(acc)
@@ -233,6 +230,22 @@
         k, e = pair // 2, pair % 2
         slot = pair % PAIRS
 
+        @pl.when((e == 0) & (k + 2 < chunks))
+        def _():
+            relay_x(k + 2)
+
+        @pl.when((e == 0) & (k + 4 < chunks))
+        def _():
+            start_z(k + 4)
+
+        @pl.when((e == 0) & (k + 1 < chunks))
+        def _():
+            relay_s(k + 1)
+
+        @pl.when(pair == 0)
+        def _():
+            relay_s(None)
+
         @pl.when(e == 0)
         def _():
             gather_s(k).wait_recv()
@@ -243,12 +256,7 @@
         for kind in range(2):
             first_copy(pair, slot, kind).wait()
 
-            @pl.loop(0, BLK // 256)
-            def _(n):
-                cols = pl.ds(pl.multiple_of(n * 256, 256), 256)
-                acc[e, kind, :, cols] += jnp.dot(
-                    xs[...], wbuf[slot, kind, :, cols], preferred_element_type=jnp.float32
-                )
+            acc[e, kind] += jnp.dot(xs[...], wbuf[slot, kind], preferred_element_type=jnp.float32)
 
         later = pair + PAIRS
 
@@ -300,14 +308,10 @@
         slot = (chunks * 2 + q) % PAIRS
         for copy in down_copies(q, slot):
             copy.wait()
-        for side in range(2):
-            for n in range(half // 256):
-                cols = slice(side * half + n * 256, side * half + (n + 1) * 256)
-                value = jnp.dot(hid[0], wbuf[slot, 0, :, cols], preferred_element_type=jnp.float32)
-                value = value + jnp.dot(hid[1], wbuf[slot, 1, :, cols], preferred_element_type=jnp.float32)
-                acc[0, side, :, n * 256 : (n + 1) * 256] = value
-        low = acc[0, 0, :, :half].reshape(2 * 2 * zs, 8, half)
-        high = acc[0, 1, :, :half].reshape(2 * 2 * zs, 8, half)
+        value = jnp.dot(hid[0], wbuf[slot, 0], preferred_element_type=jnp.float32)
+        value = value + jnp.dot(hid[1], wbuf[slot, 1], preferred_element_type=jnp.float32)
+        low = value[:, :half].reshape(2 * 2 * zs, 8, half)
+        high = value[:, half:].reshape(2 * 2 * zs, 8, half)
         part[q] = jnp.concatenate([low, high], axis=1).reshape(2, 2, zs, 16, half).astype(jnp.bfloat16)
         reduce_s(q).start()
 
@@ -333,7 +337,7 @@
                 row = side * 8 + b * 4
                 out_ref[b, :, cols] = total[row : row + 4].astype(jnp.bfloat16)
 
-    @pl.loop(0, chunks + 3)
+    @pl.loop(0, chunks + 5)
     def _(q):
         @pl.when(q < chunks)
         def _():
@@ -343,13 +347,13 @@
         def _():
             add_pair(q - 1)
 
-        @pl.when((q >= 2) & (q < chunks + 2))
-        def _():
-            add_x(q - 2)
-
-        @pl.when(q >= 3)
-        def _():
-            add_z(q - 3)
+        @pl.when((q >= 3) & (q < chunks + 3))
+        def _():
+            add_x(q - 3)
+
+        @pl.when(q >= 5)
+        def _():
+            add_z(q - 5)
 
     @pl.loop(0, chunks)
     def _(k):
@@ -384,7 +388,7 @@
         out_specs=vmem_spec,
         scratch_shapes=[
             pltpu.VMEM((PAIRS, 2, BLK, BLK), bf16),
-            pltpu.VMEM(router.shape, bf16),
+            pltpu.VMEM(router.shape[::-1], bf16),
             pltpu.VMEM((chunks, 2, 2, zs, 16, half), bf16),
             pltpu.VMEM((2, 2, zs, 16, 128), f32),
             pltpu.VMEM((rows, BLK), bf16),
@@ -411,7 +415,7 @@
         cost_estimate=pl.CostEstimate(
             flops=12 * rows * width * BLK, bytes_accessed=12 * width * BLK, transcendentals=2 * rows * BLK
         ),
-    )(tokens, node_lists, router, w_gate, w_up, w_down)
+    )(tokens, node_lists, jnp.transpose(router), w_gate, w_up, w_down)
 
 
 def solution(mesh):
@@ -423,6 +427,7 @@
             and w_gate.shape[0] == 2
             and w_gate.shape[2] == BLK
             and tokens.shape[2] % BLK == 0
+            and tokens.shape[2] // BLK >= 4
         )
         plan = fused if fits else local
         return plan(tokens, router, w_gate, w_up, w_down, node_lists)

time: 88.2 us -> 56.7 us (0.64)
  Pallas kernels: 83.9 us -> 54.9 us
  local copies, waits for them, and re-layouts: 4.09 us -> 1.59 us
    pallas_call x1, Pallas kernels: 83.9 us -> 54.9 us  [fused(): pl.pallas_call(fused_kernel, out_shape=jax.ShapeDtypeStruct(tokens.shape,...]
    unnamed x2 -> x1, local copies, waits for them, and re-layouts: 4.09 us -> 1.59 us
where the time goes in v2:
time: 56.7 us; the launch traced here: 56.5 us
  Pallas kernels  54.9 us (97%)
  local copies, waits for them, and re-layouts  1.59 us (3%)
    pallas_call x1, Pallas kernels, fused(): pl.pallas_call(fused_kernel, out_shape=jax.ShapeDtypeStruct(tokens.shape,...  54.9 us
    unnamed x1, local copies, waits for them, and re-layouts  1.59 us

profile of v2, /device:TPU:0, one launch (start us, length us, event | category | flops | bytes accessed | tf_op | source)
XLA Modules:
  0.0 56.5 jit_solution(13530272500507417214)
XLA Ops:
  0.0 54.9 %shard_map.64 = bf16[2,4,7168]{2,1,0:T(4,128)(2,1)} custom-call(bf16[2,4,7168]{2,1,0:T(4,128)(2,1)} %tok_ref.1, s32[2,4,4]{2,1,0:T(4,128)} %list_ref.1, bf16[16,7168]{1,0:T(8,128)(2,1)} %bitcast.1, bf16[2,7168,1024]{2,1,0:T(8,128)(2,1)} %gate_hbm.1, bf16[2,7168,1024]{2,1,0:T(8,128)(2,1)} %up_hbm.1, bf16[2,1024,7168]{2,1,0:T(8,128)(2,1)} %down_hbm.1), custom_call_target="tpu_custom_call" | custom-call | flops 11274289152 | bytes 88080384 | tf_op jit(solution)/shard_map/pallas_call | solution.py:384
  54.9 1.6 %copy.8 = bf16[2,4,7168]{2,1,0:T(4,128)(2,1)} copy(bf16[2,4,7168]{2,1,0:T(4,128)(2,1)} %shard_map.64) | data formatting | bytes 229376
